TPU v7x, 32 devices: a whole 2x2x4 slice. The times are simulated.
32 devices in a mesh: img: 4 (over z), gx: 2 (over x), gz: 4 (over y, core).
Axes of the slice: x: 2, y: 2, z: 4, core: 2. Of those that a mesh axis runs over, the one named last changes fastest.
Arguments:
- species: float32 [4, 2, 32, 16, 512], P('img', None, 'gx', None, 'gz'), may hold values from -2.5 to 2.5
- diffusion: float32 [2, 32, 16, 512], P(None, 'gx', None, 'gz'), may hold values from 0.1 to 2
- z_inverse: float32 [2, 512, 512], replicated, may hold values from -1 to 1.5
- starts: int32 [4], replicated, may hold values from -1 to 1, as said below
- weights: float32 [4, 4], replicated, may hold values from -0.1 to 1, as said below
Outputs:
- new_string: float32 [4, 2, 32, 16, 512], P('img', None, 'gx', None, 'gz')
Inputs may be any that keep to these rules, and one draw needn't show every extreme that they name: starts[t] is t - 2 or t - 1. Each row holds the cubic Lagrange weights at a point between the second and third of four equally spaced images.
All inputs are finite; a program needn't handle non-finite values.
Results may differ from a plain program's by a relative error of at most 0.00012.
Values sent between devices are 32-bit elements; how exact they have to be, the bound alone decides.
A program may use at most 64 MiB of HBM per device.

v0:
```python
import jax
import jax.numpy as jnp
from jax import lax
from jax.sharding import PartitionSpec as P

STEPS = 4
step_size = 0.05


def with_halo(cells, sides, width):
    for axis, dim in sides:
        count = lax.axis_size(axis)
        ends = count - 1
        head = lax.slice_in_dim(cells, 0, width, axis=dim)
        tail = lax.slice_in_dim(cells, cells.shape[dim] - width, cells.shape[dim], axis=dim)
        cells = jnp.concatenate(
            [
                lax.ppermute(tail, axis, [(i, (i + 1) % count) for i in range(ends)]),
                cells,
                lax.ppermute(head, axis, [((i + 1) % count, i) for i in range(ends)]),
            ],
            axis=dim,
        )
    return cells


def passed_along(value, axis, steps):
    count = lax.axis_size(axis)
    first, last = (max(0, -steps), min(count, count - steps))
    return lax.ppermute(value, axis, [(source, source + steps) for source in range(first, last)])


def reaction(state):
    first = state[0]
    second = state[1]
    return jnp.stack([first - first * first * first - second + 0.2, 0.5 * (first - second)])


def spread_flux(state, padded, coeffs):
    centre = coeffs[:, 1:-1, 1:-1]
    total = (centre + coeffs[:, :-2, 1:-1]) * (padded[:, :-2, 1:-1] - state)
    total = total + (centre + coeffs[:, 2:, 1:-1]) * (padded[:, 2:, 1:-1] - state)
    total = total + (centre + coeffs[:, 1:-1, :-2]) * (padded[:, 1:-1, :-2] - state)
    total = total + (centre + coeffs[:, 1:-1, 2:]) * (padded[:, 1:-1, 2:] - state)
    return 0.5 * total


def local(species, diffusion, z_inverse, starts, weights):
    state = species[0]
    y_widths = ((0, 0), (0, 0), (1, 1), (0, 0))
    coeffs = with_halo(diffusion, (("gx", 1),), 1)
    coeffs = jnp.pad(coeffs, y_widths)
    for repeat in range(STEPS):
        padded = with_halo(state, (("gx", 1),), 1)
        padded = jnp.pad(padded, y_widths)
        source = state + step_size * (reaction(state) + spread_flux(state, padded, coeffs))
        solved = jnp.einsum(
            "sij,sabj->sabi",
            z_inverse,
            lax.all_to_all(source, "gz", split_axis=2, concat_axis=3, tiled=True),
            precision=lax.Precision.HIGHEST,
        )
        state = lax.all_to_all(solved, "gz", split_axis=3, concat_axis=2, tiled=True)
    before_one = passed_along(state, "img", 1)
    before_two = passed_along(state, "img", 2)
    after_one = passed_along(state, "img", -1)
    after_two = passed_along(state, "img", -2)
    images = lax.axis_size("img")
    target = lax.axis_index("img")
    listed = jnp.arange(images, dtype=jnp.int32)
    picked = listed == target
    first_image = jnp.sum(jnp.where(picked, starts, 0))
    my_weights = jnp.sum(jnp.where(picked[:, None], weights, 0.0), axis=0)
    sources = {-2: before_two, -1: before_one, 0: state, 1: after_one, 2: after_two}
    result = None
    for offset in range(-2, 3):
        coef = jnp.zeros((), jnp.float32)
        for place in range(4):
            coef = coef + jnp.where(first_image + place == target + offset, my_weights[place], 0.0)
        term = coef * sources[offset]
        result = term if result is None else result + term
    return result[None]


def solution(mesh):
    return jax.shard_map(
        local,
        mesh=mesh,
        in_specs=(P("img", None, "gx", None, "gz"), P(None, "gx", None, "gz"), P(), P(), P()),
        out_specs=P("img", None, "gx", None, "gz"),
        check_vma=False,
    )
```

profile of v0, /device:TPU:24, one launch (start us, length us, event | category | flops | bytes accessed | tf_op | source)
XLA Modules:
  0.0 201.2 jit_solution(16023715058296012637)
XLA Ops:
  0.0 0.9 fusion.80
  0.9 3.4 %collective-permute-start = (f32[2,1,16,128]{3,1,0,2:T(1,128)S(1)}, f32[2,1,16,128]{3,1,0,2:T(1,128)S(1)}, u32[]{:S(2)}, u32[]{:S(2)}) collective-permute-start(f32[2,1,16,128]{3,1,0,2:T(1,128)S(1)} %copy.23), channel_id=1, source_target_pairs={{0,4},{1,5},{2,6},{3,7},{8,12},{9,13},{10,14},{11,15},{16,20},{17,... | collective-permute-start | bytes 49160 | tf_op jit(solution)/shard_map/ppermute | solution.py:18
  4.4 1.3 collective-permute-start.2
  5.7 1.0 copy.70
  6.7 4.5 %collective-permute-start.1 = (f32[2,1,16,128]{3,1,0,2:T(1,128)S(1)}, f32[2,1,16,128]{3,1,0,2:T(1,128)S(1)}, u32[]{:S(2)}, u32[]{:S(2)}) collective-permute-start(f32[2,1,16,128]{3,1,0,2:T(1,128)S(1)} %get-tuple-element.32), channel_id=1, source_target_pairs={{0,4},{1,5},{2,6},{3,7},{8,12},{9,13},{10,14},{11,15},{16,20},{17,... | collective-permute-start | bytes 49160 | tf_op jit(solution)/shard_map/ppermute | solution.py:18
  11.3 1.3 collective-permute-start.3
  12.6 1.0 fusion.81
  13.7 1.0 copy.25
  14.7 2.2 %collective-permute-done.3 = f32[2,1,16,128]{3,1,0,2:T(1,128)S(1)} collective-permute-done((f32[2,1,16,128]{3,1,0,2:T(1,128)S(1)}, f32[2,1,16,128]{3,1,0,2:T(1,128)S(1)}, u32[]{:S(2)}, u32[]{:S(2)}) %collective-permute-start.3) | collective-permute-done | bytes 16416 | tf_op jit(solution)/shard_map/ppermute | solution.py:20
  17.5 8.6 %all_to_all.144 = f32[2,16,16,128]{3,1,0,2:T(8,128)S(1)} all-to-all(f32[2,16,16,128]{3,1,0,2:T(8,128)S(1)} %get-tuple-element.5), channel_id=1, replica_groups=mesh['img'=4,'gx'=2,'gz'=4] {'gz'}, dimensions={2} | all-to-all | bytes 524288 | tf_op jit(solution)/shard_map/all_to_all | solution.py:60
  26.1 0.9 copy.69
  27.0 1.1 all_to_all.107
  28.0 2.1 %fusion.6 = f32[2,16,4,512]{3,1,2,0:T(8,128)S(1)} fusion(f32[2,16,4,512]{3,1,2,0:T(8,128)S(1)} %all_to_all.107, f32[2,512,512]{2,1,0:T(8,128)S(1)} %copy-done), kind=kOutput, calls=%fused_computation.6 | convolution fusion | flops 402653184 | bytes 2621440 | tf_op jit(solution)/shard_map/sij,sabj->sabi/dot_general | solution.py:57
  30.2 1.7 copy.33
  31.9 3.1 %reshape.265 = f32[4,1,16384]{2,1,0:T(1,128)S(1)} reshape(f32[512,2,4,16]{3,2,1,0:T(4,128)} %bitcast.108) | data formatting | bytes 524288
  35.0 8.4 %all_to_all.145 = f32[4,1,16384]{2,1,0:T(1,128)S(1)} all-to-all(f32[4,1,16384]{2,1,0:T(1,128)S(1)} %reshape.265), channel_id=1, replica_groups=mesh['img'=4,'gx'=2,'gz'=4] {'gz'}, dimensions={0} | all-to-all | bytes 524288 | tf_op jit(solution)/shard_map/all_to_all | solution.py:63
  44.0 1.4 reduce
  45.4 2.9 %reshape.266 = f32[512,2,4,16]{3,2,1,0:T(4,128)} reshape(f32[4,16384]{1,0:T(4,128)S(1)} %reduce) | data formatting | bytes 524288
  48.3 1.8 copy.34
  50.1 2.4 %collective-permute-start.4 = (f32[2,1,16,128]{3,1,0,2:T(1,128)S(1)}, f32[2,1,16,128]{3,1,0,2:T(1,128)S(1)}, u32[]{:S(2)}, u32[]{:S(2)}) collective-permute-start(f32[2,1,16,128]{3,1,0,2:T(1,128)S(1)} %get-tuple-element.24), channel_id=1, source_target_pairs={{0,4},{1,5},{2,6},{3,7},{8,12},{9,13},{10,14},{11,15},{16,20},{17,... | collective-permute-start | bytes 49160 | tf_op jit(solution)/shard_map/ppermute | solution.py:18
  52.5 1.3 collective-permute-start.5
  53.9 4.2 %collective-permute-done.5 = f32[2,1,16,128]{3,1,0,2:T(1,128)S(1)} collective-permute-done((f32[2,1,16,128]{3,1,0,2:T(1,128)S(1)}, f32[2,1,16,128]{3,1,0,2:T(1,128)S(1)}, u32[]{:S(2)}, u32[]{:S(2)}) %collective-permute-start.5) | collective-permute-done | bytes 16416 | tf_op jit(solution)/shard_map/ppermute | solution.py:20
  58.5 8.4 %all_to_all.146 = f32[2,16,16,128]{3,1,0,2:T(8,128)S(1)} all-to-all(f32[2,16,16,128]{3,1,0,2:T(8,128)S(1)} %fusion.40), channel_id=1, replica_groups=mesh['img'=4,'gx'=2,'gz'=4] {'gz'}, dimensions={2} | all-to-all | bytes 524288 | tf_op jit(solution)/shard_map/all_to_all | solution.py:60
  67.0 0.9 copy.68
  67.8 1.1 all_to_all.115
  68.9 2.1 %fusion.4 = f32[2,16,4,512]{3,1,2,0:T(8,128)S(1)} fusion(f32[2,16,4,512]{3,1,2,0:T(8,128)S(1)} %all_to_all.115, f32[2,512,512]{2,1,0:T(8,128)S(1)} %copy-done), kind=kOutput, calls=%fused_computation.4 | convolution fusion | flops 402653184 | bytes 2621440 | tf_op jit(solution)/shard_map/sij,sabj->sabi/dot_general | solution.py:57
  71.0 1.7 copy.36
  72.8 3.1 %reshape.267 = f32[4,1,16384]{2,1,0:T(1,128)S(1)} reshape(f32[512,2,4,16]{3,2,1,0:T(4,128)} %bitcast.110) | data formatting | bytes 524288
  75.8 8.4 %all_to_all.147 = f32[4,1,16384]{2,1,0:T(1,128)S(1)} all-to-all(f32[4,1,16384]{2,1,0:T(1,128)S(1)} %reshape.267), channel_id=1, replica_groups=mesh['img'=4,'gx'=2,'gz'=4] {'gz'}, dimensions={0} | all-to-all | bytes 524288 | tf_op jit(solution)/shard_map/all_to_all | solution.py:63
  84.3 1.4 reduce.1
  85.7 2.9 %reshape.268 = f32[512,2,4,16]{3,2,1,0:T(4,128)} reshape(f32[4,16384]{1,0:T(4,128)S(1)} %reduce.1) | data formatting | bytes 524288
  88.5 1.8 copy.37
  90.4 1.6 collective-permute-start.6
  92.1 1.3 collective-permute-start.7
  93.5 4.2 %collective-permute-done.7 = f32[2,1,16,128]{3,1,0,2:T(1,128)S(1)} collective-permute-done((f32[2,1,16,128]{3,1,0,2:T(1,128)S(1)}, f32[2,1,16,128]{3,1,0,2:T(1,128)S(1)}, u32[]{:S(2)}, u32[]{:S(2)}) %collective-permute-start.7) | collective-permute-done | bytes 16416 | tf_op jit(solution)/shard_map/ppermute | solution.py:20
  98.1 8.4 %all_to_all.148 = f32[2,16,16,128]{3,1,0,2:T(8,128)S(1)} all-to-all(f32[2,16,16,128]{3,1,0,2:T(8,128)S(1)} %fusion.27), channel_id=1, replica_groups=mesh['img'=4,'gx'=2,'gz'=4] {'gz'}, dimensions={2} | all-to-all | bytes 524288 | tf_op jit(solution)/shard_map/all_to_all | solution.py:60
  106.5 0.9 copy.67
  107.4 1.1 all_to_all.123
  108.4 2.1 %fusion.2 = f32[2,16,4,512]{3,1,2,0:T(8,128)S(1)} fusion(f32[2,16,4,512]{3,1,2,0:T(8,128)S(1)} %all_to_all.123, f32[2,512,512]{2,1,0:T(8,128)S(1)} %copy-done), kind=kOutput, calls=%fused_computation.2 | convolution fusion | flops 402653184 | bytes 2621440 | tf_op jit(solution)/shard_map/sij,sabj->sabi/dot_general | solution.py:57
  110.6 1.7 copy.39
  112.3 3.1 %reshape.269 = f32[4,1,16384]{2,1,0:T(1,128)S(1)} reshape(f32[512,2,4,16]{3,2,1,0:T(4,128)} %bitcast.112) | data formatting | bytes 524288
  115.4 8.4 %all_to_all.149 = f32[4,1,16384]{2,1,0:T(1,128)S(1)} all-to-all(f32[4,1,16384]{2,1,0:T(1,128)S(1)} %reshape.269), channel_id=1, replica_groups=mesh['img'=4,'gx'=2,'gz'=4] {'gz'}, dimensions={0} | all-to-all | bytes 524288 | tf_op jit(solution)/shard_map/all_to_all | solution.py:63
  123.8 1.4 reduce.2
  125.2 2.9 %reshape.270 = f32[512,2,4,16]{3,2,1,0:T(4,128)} reshape(f32[4,16384]{1,0:T(4,128)S(1)} %reduce.2) | data formatting | bytes 524288
  128.1 1.8 copy.40
  130.0 1.6 collective-permute-start.8
  131.6 1.3 collective-permute-start.9
  133.1 4.2 %collective-permute-done.9 = f32[2,1,16,128]{3,1,0,2:T(1,128)S(1)} collective-permute-done((f32[2,1,16,128]{3,1,0,2:T(1,128)S(1)}, f32[2,1,16,128]{3,1,0,2:T(1,128)S(1)}, u32[]{:S(2)}, u32[]{:S(2)}) %collective-permute-start.9) | collective-permute-done | bytes 16416 | tf_op jit(solution)/shard_map/ppermute | solution.py:20
  137.6 8.4 %all_to_all.150 = f32[2,16,16,128]{3,1,0,2:T(8,128)S(1)} all-to-all(f32[2,16,16,128]{3,1,0,2:T(8,128)S(1)} %fusion.14), channel_id=1, replica_groups=mesh['img'=4,'gx'=2,'gz'=4] {'gz'}, dimensions={2} | all-to-all | bytes 524288 | tf_op jit(solution)/shard_map/all_to_all | solution.py:60
  146.3 2.1 %fusion = f32[2,16,4,512]{3,1,2,0:T(8,128)S(1)} fusion(f32[2,16,4,512]{3,1,2,0:T(8,128)S(1)} %all_to_all.131, f32[2,512,512]{2,1,0:T(8,128)S(1)} %copy-done), kind=kOutput, calls=%fused_computation | convolution fusion | flops 402653184 | bytes 2621440 | tf_op jit(solution)/shard_map/sij,sabj->sabi/dot_general | solution.py:57
  148.5 1.7 copy.42
  150.2 3.7 %reshape.271 = f32[4,1,16384]{2,1,0:T(1,128)} reshape(f32[512,2,4,16]{3,2,1,0:T(4,128)} %bitcast.114) | data formatting | bytes 524288
  153.9 3.4 %all-to-all-start.7 = ((f32[4,1,16384]{2,1,0:T(1,128)}), f32[4,1,16384]{2,1,0:T(1,128)S(1)}, u32[]{:S(2)}, u32[]{:S(2)}) async-start(f32[4,1,16384]{2,1,0:T(1,128)} %reshape.271), calls=%async_computation.7 | async-start | bytes 524288 | tf_op jit(solution)/shard_map/all_to_all | solution.py:63
  157.4 0.6 select_reduce_fusion.1
  158.0 5.4 %all-to-all-done.7 = f32[4,1,16384]{2,1,0:T(1,128)S(1)} async-done(((f32[4,1,16384]{2,1,0:T(1,128)}), f32[4,1,16384]{2,1,0:T(1,128)S(1)}, u32[]{:S(2)}, u32[]{:S(2)}) %all-to-all-start.7) | async-done | bytes 262176 | tf_op jit(solution)/shard_map/all_to_all | solution.py:63
  163.3 1.4 reduce.3
  164.8 2.9 %reshape.272 = f32[512,2,4,16]{3,2,1,0:T(4,128)} reshape(f32[4,16384]{1,0:T(4,128)S(1)} %reduce.3) | data formatting | bytes 524288
  167.6 1.9 copy.43
  169.5 1.3 collective-permute-start.10
  170.8 1.3 collective-permute-start.11
  172.1 4.6 %collective-permute-start.12 = (f32[2,16,16,128]{3,2,1,0:T(8,128)S(1)}, f32[2,16,16,128]{3,2,1,0:T(8,128)S(1)}, u32[]{:S(2)}, u32[]{:S(2)}) collective-permute-start(f32[2,16,16,128]{3,2,1,0:T(8,128)S(1)} %bitcast.133), channel_id=1, source_target_pairs={{8,0},{16,8},{24,16},{9,1},{17,9},{25,17},{10,2},{18,10},{26,18},{... | collective-permute-start | bytes 786440 | tf_op jit(solution)/shard_map/ppermute | solution.py:30
  176.7 5.5 %collective-permute-start.13 = (f32[2,16,16,128]{3,2,1,0:T(8,128)S(1)}, f32[2,16,16,128]{3,2,1,0:T(8,128)S(1)}, u32[]{:S(2)}, u32[]{:S(2)}) collective-permute-start(f32[2,16,16,128]{3,2,1,0:T(8,128)S(1)} %bitcast.134), channel_id=1, source_target_pairs={{16,0},{24,8},{17,1},{25,9},{18,2},{26,10},{19,3},{27,11},{20,4},{... | collective-permute-start | bytes 786440 | tf_op jit(solution)/shard_map/ppermute | solution.py:30
  186.8 0.7 fusion.83
  200.4 0.8 add_bitcast_fusion
  (45 shorter events, 3.3 us)
Async XLA Ops:
  0.0 28.0 %copy-start = (f32[2,512,512]{2,1,0:T(8,128)S(1)}, f32[2,512,512]{2,1,0:T(8,128)}, u32[]{:S(2)}) copy-start(f32[2,512,512]{2,1,0:T(8,128)} %param.7) | copy-start | bytes 6291460
  0.0 17.1 %copy-start.1 = (f32[2,16,16,128]{3,2,1,0:T(8,128)S(1)}, f32[2,16,16,128]{3,2,1,0:T(8,128)}, u32[]{:S(2)}) copy-start(f32[2,16,16,128]{3,2,1,0:T(8,128)} %param.6) | copy-start | bytes 786436
  0.9 16.1 %collective-permute-start = (f32[2,1,16,128]{3,1,0,2:T(1,128)S(1)}, f32[2,1,16,128]{3,1,0,2:T(1,128)S(1)}, u32[]{:S(2)}, u32[]{:S(2)}) collective-permute-start(f32[2,1,16,128]{3,1,0,2:T(1,128)S(1)} %copy.23), channel_id=1, source_target_pairs={{0,4},{1,5},{2,6},{3,7},{8,12},{9,13},{10,14},{11,15},{16,20},{17,... | collective-permute-start | bytes 49160 | tf_op jit(solution)/shard_map/ppermute | solution.py:18
  4.4 12.6 %collective-permute-start.2 = (f32[2,1,16,128]{3,1,0,2:T(1,128)S(1)}, f32[2,1,16,128]{3,1,0,2:T(1,128)S(1)}, u32[]{:S(2)}, u32[]{:S(2)}) collective-permute-start(f32[2,1,16,128]{3,1,0,2:T(1,128)S(1)} %copy.26), channel_id=1, source_target_pairs={{4,0},{5,1},{6,2},{7,3},{12,8},{13,9},{14,10},{15,11},{20,16},{21,... | collective-permute-start | bytes 49160 | tf_op jit(solution)/shard_map/ppermute | solution.py:20
  6.7 8.0 %collective-permute-start.1 = (f32[2,1,16,128]{3,1,0,2:T(1,128)S(1)}, f32[2,1,16,128]{3,1,0,2:T(1,128)S(1)}, u32[]{:S(2)}, u32[]{:S(2)}) collective-permute-start(f32[2,1,16,128]{3,1,0,2:T(1,128)S(1)} %get-tuple-element.32), channel_id=1, source_target_pairs={{0,4},{1,5},{2,6},{3,7},{8,12},{9,13},{10,14},{11,15},{16,20},{17,... | collective-permute-start | bytes 49160 | tf_op jit(solution)/shard_map/ppermute | solution.py:18
  11.3 5.6 %collective-permute-start.3 = (f32[2,1,16,128]{3,1,0,2:T(1,128)S(1)}, f32[2,1,16,128]{3,1,0,2:T(1,128)S(1)}, u32[]{:S(2)}, u32[]{:S(2)}) collective-permute-start(f32[2,1,16,128]{3,1,0,2:T(1,128)S(1)} %get-tuple-element.33), channel_id=1, source_target_pairs={{4,0},{5,1},{6,2},{7,3},{12,8},{13,9},{14,10},{15,11},{20,16},{21,... | collective-permute-start | bytes 49160 | tf_op jit(solution)/shard_map/ppermute | solution.py:20
  50.1 3.8 %collective-permute-start.4 = (f32[2,1,16,128]{3,1,0,2:T(1,128)S(1)}, f32[2,1,16,128]{3,1,0,2:T(1,128)S(1)}, u32[]{:S(2)}, u32[]{:S(2)}) collective-permute-start(f32[2,1,16,128]{3,1,0,2:T(1,128)S(1)} %get-tuple-element.24), channel_id=1, source_target_pairs={{0,4},{1,5},{2,6},{3,7},{8,12},{9,13},{10,14},{11,15},{16,20},{17,... | collective-permute-start | bytes 49160 | tf_op jit(solution)/shard_map/ppermute | solution.py:18
  52.5 5.6 %collective-permute-start.5 = (f32[2,1,16,128]{3,1,0,2:T(1,128)S(1)}, f32[2,1,16,128]{3,1,0,2:T(1,128)S(1)}, u32[]{:S(2)}, u32[]{:S(2)}) collective-permute-start(f32[2,1,16,128]{3,1,0,2:T(1,128)S(1)} %get-tuple-element.25), channel_id=1, source_target_pairs={{4,0},{5,1},{6,2},{7,3},{12,8},{13,9},{14,10},{15,11},{20,16},{21,... | collective-permute-start | bytes 49160 | tf_op jit(solution)/shard_map/ppermute | solution.py:20
  90.4 3.1 %collective-permute-start.6 = (f32[2,1,16,128]{3,1,0,2:T(1,128)S(1)}, f32[2,1,16,128]{3,1,0,2:T(1,128)S(1)}, u32[]{:S(2)}, u32[]{:S(2)}) collective-permute-start(f32[2,1,16,128]{3,1,0,2:T(1,128)S(1)} %get-tuple-element.18), channel_id=1, source_target_pairs={{0,4},{1,5},{2,6},{3,7},{8,12},{9,13},{10,14},{11,15},{16,20},{17,... | collective-permute-start | bytes 49160 | tf_op jit(solution)/shard_map/ppermute | solution.py:18
  92.1 5.6 %collective-permute-start.7 = (f32[2,1,16,128]{3,1,0,2:T(1,128)S(1)}, f32[2,1,16,128]{3,1,0,2:T(1,128)S(1)}, u32[]{:S(2)}, u32[]{:S(2)}) collective-permute-start(f32[2,1,16,128]{3,1,0,2:T(1,128)S(1)} %get-tuple-element.19), channel_id=1, source_target_pairs={{4,0},{5,1},{6,2},{7,3},{12,8},{13,9},{14,10},{15,11},{20,16},{21,... | collective-permute-start | bytes 49160 | tf_op jit(solution)/shard_map/ppermute | solution.py:20
  130.0 3.1 %collective-permute-start.8 = (f32[2,1,16,128]{3,1,0,2:T(1,128)S(1)}, f32[2,1,16,128]{3,1,0,2:T(1,128)S(1)}, u32[]{:S(2)}, u32[]{:S(2)}) collective-permute-start(f32[2,1,16,128]{3,1,0,2:T(1,128)S(1)} %get-tuple-element.12), channel_id=1, source_target_pairs={{0,4},{1,5},{2,6},{3,7},{8,12},{9,13},{10,14},{11,15},{16,20},{17,... | collective-permute-start | bytes 49160 | tf_op jit(solution)/shard_map/ppermute | solution.py:18
  131.6 5.6 %collective-permute-start.9 = (f32[2,1,16,128]{3,1,0,2:T(1,128)S(1)}, f32[2,1,16,128]{3,1,0,2:T(1,128)S(1)}, u32[]{:S(2)}, u32[]{:S(2)}) collective-permute-start(f32[2,1,16,128]{3,1,0,2:T(1,128)S(1)} %get-tuple-element.13), channel_id=1, source_target_pairs={{4,0},{5,1},{6,2},{7,3},{12,8},{13,9},{14,10},{15,11},{20,16},{21,... | collective-permute-start | bytes 49160 | tf_op jit(solution)/shard_map/ppermute | solution.py:20
  148.5 8.9 %copy-start.3 = (s32[4]{0:T(128)S(1)}, s32[4]{0:T(128)}, u32[]{:S(2)}) copy-start(s32[4]{0:T(128)} %param.8) | copy-start | bytes 52
  153.9 9.4 %all-to-all-start.7 = ((f32[4,1,16384]{2,1,0:T(1,128)}), f32[4,1,16384]{2,1,0:T(1,128)S(1)}, u32[]{:S(2)}, u32[]{:S(2)}) async-start(f32[4,1,16384]{2,1,0:T(1,128)} %reshape.271), calls=%async_computation.7 | async-start | bytes 524288 | tf_op jit(solution)/shard_map/all_to_all | solution.py:63
  164.8 22.0 %copy-start.2 = (f32[4,4]{1,0:T(4,128)S(1)}, f32[4,4]{1,0:T(4,128)}, u32[]{:S(2)}) copy-start(f32[4,4]{1,0:T(4,128)} %param.9) | copy-start | bytes 196
  169.5 30.8 %collective-permute-start.10 = (f32[2,16,16,128]{3,2,1,0:T(8,128)S(1)}, f32[2,16,16,128]{3,2,1,0:T(8,128)S(1)}, u32[]{:S(2)}, u32[]{:S(2)}) collective-permute-start(f32[2,16,16,128]{3,2,1,0:T(8,128)S(1)} %bitcast.131), channel_id=1, source_target_pairs={{0,16},{8,24},{1,17},{9,25},{2,18},{10,26},{3,19},{11,27},{4,20},{... | collective-permute-start | bytes 786440 | tf_op jit(solution)/shard_map/ppermute | solution.py:30
  170.8 29.5 %collective-permute-start.11 = (f32[2,16,16,128]{3,2,1,0:T(8,128)S(1)}, f32[2,16,16,128]{3,2,1,0:T(8,128)S(1)}, u32[]{:S(2)}, u32[]{:S(2)}) collective-permute-start(f32[2,16,16,128]{3,2,1,0:T(8,128)S(1)} %bitcast.132), channel_id=1, source_target_pairs={{0,8},{8,16},{16,24},{1,9},{9,17},{17,25},{2,10},{10,18},{18,26},{... | collective-permute-start | bytes 786440 | tf_op jit(solution)/shard_map/ppermute | solution.py:30
  172.1 28.2 %collective-permute-start.12 = (f32[2,16,16,128]{3,2,1,0:T(8,128)S(1)}, f32[2,16,16,128]{3,2,1,0:T(8,128)S(1)}, u32[]{:S(2)}, u32[]{:S(2)}) collective-permute-start(f32[2,16,16,128]{3,2,1,0:T(8,128)S(1)} %bitcast.133), channel_id=1, source_target_pairs={{8,0},{16,8},{24,16},{9,1},{17,9},{25,17},{10,2},{18,10},{26,18},{... | collective-permute-start | bytes 786440 | tf_op jit(solution)/shard_map/ppermute | solution.py:30
  176.7 23.7 %collective-permute-start.13 = (f32[2,16,16,128]{3,2,1,0:T(8,128)S(1)}, f32[2,16,16,128]{3,2,1,0:T(8,128)S(1)}, u32[]{:S(2)}, u32[]{:S(2)}) collective-permute-start(f32[2,16,16,128]{3,2,1,0:T(8,128)S(1)} %bitcast.134), channel_id=1, source_target_pairs={{16,0},{24,8},{17,1},{25,9},{18,2},{26,10},{19,3},{27,11},{20,4},{... | collective-permute-start | bytes 786440 | tf_op jit(solution)/shard_map/ppermute | solution.py:30
where the time goes:
time: 203 us; the launch traced here: 201 us
  blocking collectives  59.2 us (29%)
  local copies, waits for them, and re-layouts  50.2 us (25%)
  starting transfers between devices  36.1 us (18%)
  waiting for transfers between devices  20.4 us (10%)
  between operations  17.8 us (9%)
  other arithmetic  8.99 us (4%)
  matrix products  8.52 us (4%)
    all_to_all x4, blocking collectives, local(): lax.all_to_all(source, 'gz', split_axis=2, concat_axis=3, tiled=True)  33.9 us
    unnamed x18, local copies, waits for them, and re-layouts  26.4 us
    all_to_all x3, blocking collectives, local(): lax.all_to_all(solved, 'gz', split_axis=3, concat_axis=2, tiled=True)  25.3 us
    ppermute x5, waiting for transfers between devices, with_halo(): lax.ppermute(head, axis, [((i + 1) % count, i) for i in range(ends)])  14.8 us
    ppermute x5, starting transfers between devices, with_halo(): lax.ppermute(tail, axis, [(i, (i + 1) % count) for i in range(ends)])  13.6 us
    ppermute x4, starting transfers between devices, passed_along(): lax.ppermute(value, axis, [(source, source + steps) for source in range(f...  12.6 us
    dot_general x4, matrix products, local(): jnp.einsum('sij,sabj->sabi', z_inverse, lax.all_to_all(source, 'gz', spli...  8.52 us
    all_to_all x5, local copies, waits for them, and re-layouts, local(): lax.all_to_all(solved, 'gz', split_axis=3, concat_axis=2, tiled=True)  7.99 us
  transfers between devices with their start and end apart: 15, of which 8 were waited for; matrix products, arithmetic and copies ran while one was open for 2% of the time, Pallas kernels for 0%

commit v1 on v0

--- a/solution.py
+++ b/solution.py
@@ -60,7 +60,19 @@
             lax.all_to_all(source, "gz", split_axis=2, concat_axis=3, tiled=True),
             precision=lax.Precision.HIGHEST,
         )
-        state = lax.all_to_all(solved, "gz", split_axis=3, concat_axis=2, tiled=True)
+        ways, here = (lax.axis_size("gz"), lax.axis_index("gz"))
+        width_2 = solved.shape[3] // ways
+        shape = list(solved.shape)
+        shape[3] = width_2
+        height = shape[2]
+        shape[2] = height * ways
+        full = jnp.zeros(shape, solved.dtype)
+        for mask in range(ways):
+            part = lax.dynamic_slice_in_dim(solved, (here ^ mask) * width_2, width_2, axis=3)
+            if mask:
+                part = lax.ppermute(part, "gz", [(d, d ^ mask) for d in range(ways)])
+            full = lax.dynamic_update_slice_in_dim(full, part, (here ^ mask) * height, axis=2)
+        state = full
     before_one = passed_along(state, "img", 1)
     before_two = passed_along(state, "img", 2)
     after_one = passed_along(state, "img", -1)

time: 203 us -> 143 us (0.70)
  local copies, waits for them, and re-layouts: 50.2 us -> 7.14 us
  blocking collectives: 59.2 us -> 16.8 us
  waiting for transfers between devices: 20.4 us -> 40.2 us
  starting transfers between devices: 36.1 us -> 47.4 us
  other arithmetic: 8.99 us -> 4.14 us
    all_to_all x3 -> x0, blocking collectives: 25.3 us -> none  [local(): lax.all_to_all(solved, 'gz', split_axis=3, concat_axis=2, tiled=True)]
    unnamed x18 -> x10, local copies, waits for them, and re-layouts: 26.4 us -> 2.1 us
    all_to_all x4 -> x2, blocking collectives: 33.9 us -> 16.8 us  [local(): lax.all_to_all(source, 'gz', split_axis=2, concat_axis=3, tiled=True)]
    ppermute x0 -> x12, waiting for transfers between devices: none -> 14 us  [local(): part = lax.ppermute(part, 'gz', [(d, d ^ mask) for d in range(ways)])]
    all_to_all x5 -> x0, local copies, waits for them, and re-layouts: 7.99 us -> none  [local(): lax.all_to_all(solved, 'gz', split_axis=3, concat_axis=2, tiled=True)]
    ppermute x0 -> x12, starting transfers between devices: none -> 7.73 us  [local(): part = lax.ppermute(part, 'gz', [(d, d ^ mask) for d in range(ways)])]
    dot_general x4 -> x0, local copies, waits for them, and re-layouts: 6.95 us -> none  [local(): jnp.einsum('sij,sabj->sabi', z_inverse, lax.all_to_all(source, 'gz', spli...]
    all_to_all x1 -> x2, waiting for transfers between devices: 5.36 us -> 11.1 us  [local(): lax.all_to_all(source, 'gz', split_axis=2, concat_axis=3, tiled=True)]
  transfers between devices with their start and end apart: 15 -> 28, of which waited for: 8 -> 17; matrix products, arithmetic and copies ran while one was open for 2% -> 3% of each run, Pallas kernels for 0% -> 0%
where the time goes in v1:
time: 143 us; the launch traced here: 142 us
  starting transfers between devices  47.4 us (33%)
  waiting for transfers between devices  40.2 us (28%)
  between operations  18.1 us (13%)
  blocking collectives  16.8 us (12%)
  matrix products  8.52 us (6%)
  local copies, waits for them, and re-layouts  7.14 us (5%)
  other arithmetic  4.14 us (3%)
    all_to_all x2, blocking collectives, local(): lax.all_to_all(source, 'gz', split_axis=2, concat_axis=3, tiled=True)  16.8 us
    ppermute x5, waiting for transfers between devices, with_halo(): lax.ppermute(head, axis, [((i + 1) % count, i) for i in range(ends)])  14.8 us
    ppermute x12, waiting for transfers between devices, local(): part = lax.ppermute(part, 'gz', [(d, d ^ mask) for d in range(ways)])  14 us
    ppermute x5, starting transfers between devices, with_halo(): lax.ppermute(tail, axis, [(i, (i + 1) % count) for i in range(ends)])  13.6 us
    ppermute x4, starting transfers between devices, passed_along(): lax.ppermute(value, axis, [(source, source + steps) for source in range(f...  12.6 us
    all_to_all x2, waiting for transfers between devices, local(): lax.all_to_all(source, 'gz', split_axis=2, concat_axis=3, tiled=True)  11.1 us
    dot_general x4, matrix products, local(): jnp.einsum('sij,sabj->sabi', z_inverse, lax.all_to_all(source, 'gz', spli...  8.52 us
    ppermute x12, starting transfers between devices, local(): part = lax.ppermute(part, 'gz', [(d, d ^ mask) for d in range(ways)])  7.73 us
  transfers between devices with their start and end apart: 28, of which 17 were waited for; matrix products, arithmetic and copies ran while one was open for 3% of the time, Pallas kernels for 0%

profile of v1, /device:TPU:24, one launch (start us, length us, event | category | flops | bytes accessed | tf_op | source)
XLA Modules:
  0.0 142.3 jit_solution(11270501871440233423)
XLA Ops:
  0.0 0.9 fusion.74
  0.9 3.4 %collective-permute-start = (f32[2,1,16,128]{3,1,0,2:T(1,128)S(1)}, f32[2,1,16,128]{3,1,0,2:T(1,128)S(1)}, u32[]{:S(2)}, u32[]{:S(2)}) collective-permute-start(f32[2,1,16,128]{3,1,0,2:T(1,128)S(1)} %copy.29), channel_id=1, source_target_pairs={{0,4},{1,5},{2,6},{3,7},{8,12},{9,13},{10,14},{11,15},{16,20},{17,... | collective-permute-start | bytes 49160 | tf_op jit(solution)/shard_map/ppermute | solution.py:18
  4.4 1.3 collective-permute-start.2
  5.7 1.0 copy.101
  6.7 4.5 %collective-permute-start.1 = (f32[2,1,16,128]{3,1,0,2:T(1,128)S(1)}, f32[2,1,16,128]{3,1,0,2:T(1,128)S(1)}, u32[]{:S(2)}, u32[]{:S(2)}) collective-permute-start(f32[2,1,16,128]{3,1,0,2:T(1,128)S(1)} %get-tuple-element.42), channel_id=1, source_target_pairs={{0,4},{1,5},{2,6},{3,7},{8,12},{9,13},{10,14},{11,15},{16,20},{17,... | collective-permute-start | bytes 49160 | tf_op jit(solution)/shard_map/ppermute | solution.py:18
  11.3 1.3 collective-permute-start.3
  12.6 1.0 fusion.75
  13.7 1.0 copy.31
  14.7 2.2 %collective-permute-done.3 = f32[2,1,16,128]{3,1,0,2:T(1,128)S(1)} collective-permute-done((f32[2,1,16,128]{3,1,0,2:T(1,128)S(1)}, f32[2,1,16,128]{3,1,0,2:T(1,128)S(1)}, u32[]{:S(2)}, u32[]{:S(2)}) %collective-permute-start.3) | collective-permute-done | bytes 16416 | tf_op jit(solution)/shard_map/ppermute | solution.py:20
  17.1 1.1 fusion.53
  18.2 3.4 %all-to-all-start = ((f32[2,16,16,128]{3,1,0,2:T(8,128)}), f32[2,16,16,128]{3,1,0,2:T(8,128)S(1)}, u32[]{:S(2)}, u32[]{:S(2)}) async-start(f32[2,16,16,128]{3,1,0,2:T(8,128)} %get-tuple-element.5), calls=%async_computation | async-start | bytes 524288 | tf_op jit(solution)/shard_map/all_to_all | solution.py:60
  21.6 6.0 %all-to-all-done = f32[2,16,16,128]{3,1,0,2:T(8,128)S(1)} async-done(((f32[2,16,16,128]{3,1,0,2:T(8,128)}), f32[2,16,16,128]{3,1,0,2:T(8,128)S(1)}, u32[]{:S(2)}, u32[]{:S(2)}) %all-to-all-start) | async-done | bytes 262176 | tf_op jit(solution)/shard_map/all_to_all | solution.py:60
  27.6 0.2 copy.100
  27.7 0.1 all_to_all.55
  27.9 2.1 %fusion.6 = f32[2,16,4,512]{3,1,2,0:T(8,128)S(1)} fusion(f32[2,16,4,512]{3,1,2,0:T(8,128)S(1)} %all_to_all.55, f32[2,512,512]{2,1,0:T(8,128)S(1)} %copy-done), kind=kOutput, calls=%fused_computation.6 | convolution fusion | flops 402653184 | bytes 2621440 | tf_op jit(solution)/shard_map/sij,sabj->sabi/dot_general | solution.py:57
  30.1 0.4 collective-permute-start.5
  30.6 1.4 %collective-permute-start.6 = (f32[2,16,4,128]{3,1,2,0:T(8,128)S(1)}, f32[2,16,4,128]{3,1,2,0:T(8,128)S(1)}, u32[]{:S(2)}, u32[]{:S(2)}) collective-permute-start(f32[2,16,4,128]{3,1,2,0:T(8,128)S(1)} %get-tuple-element.32), channel_id=1, source_target_pairs={{0,3},{1,2},{2,1},{3,0},{4,7},{5,6},{6,5},{7,4},{8,11},{9,10},{10,... | collective-permute-start | bytes 196616 | tf_op jit(solution)/shard_map/ppermute | solution.py:73
  32.1 3.0 %collective-permute-done.5 = f32[2,16,4,128]{3,1,2,0:T(8,128)S(1)} collective-permute-done((f32[2,16,4,128]{3,1,2,0:T(8,128)S(1)}, f32[2,16,4,128]{3,1,2,0:T(8,128)S(1)}, u32[]{:S(2)}, u32[]{:S(2)}) %collective-permute-start.5) | collective-permute-done | bytes 65568 | tf_op jit(solution)/shard_map/ppermute | solution.py:73
  35.1 0.5 collective-permute-done.6
  35.6 2.4 %collective-permute-start.7 = (f32[2,1,16,128]{3,1,0,2:T(1,128)S(1)}, f32[2,1,16,128]{3,1,0,2:T(1,128)S(1)}, u32[]{:S(2)}, u32[]{:S(2)}) collective-permute-start(f32[2,1,16,128]{3,1,0,2:T(1,128)S(1)} %get-tuple-element.30), channel_id=1, source_target_pairs={{0,4},{1,5},{2,6},{3,7},{8,12},{9,13},{10,14},{11,15},{16,20},{17,... | collective-permute-start | bytes 49160 | tf_op jit(solution)/shard_map/ppermute | solution.py:18
  38.0 1.3 collective-permute-start.8
  39.4 4.2 %collective-permute-done.8 = f32[2,1,16,128]{3,1,0,2:T(1,128)S(1)} collective-permute-done((f32[2,1,16,128]{3,1,0,2:T(1,128)S(1)}, f32[2,1,16,128]{3,1,0,2:T(1,128)S(1)}, u32[]{:S(2)}, u32[]{:S(2)}) %collective-permute-start.8) | collective-permute-done | bytes 16416 | tf_op jit(solution)/shard_map/ppermute | solution.py:20
  43.7 0.3 fusion.40
  44.0 8.4 %all_to_all.72 = f32[2,16,16,128]{3,1,0,2:T(8,128)S(1)} all-to-all(f32[2,16,16,128]{3,1,0,2:T(8,128)S(1)} %fusion.40), channel_id=1, replica_groups=mesh['img'=4,'gx'=2,'gz'=4] {'gz'}, dimensions={2} | all-to-all | bytes 524288 | tf_op jit(solution)/shard_map/all_to_all | solution.py:60
  52.5 0.2 copy.99
  52.6 0.1 all_to_all.59
  52.7 2.1 %fusion.4 = f32[2,16,4,512]{3,1,2,0:T(8,128)S(1)} fusion(f32[2,16,4,512]{3,1,2,0:T(8,128)S(1)} %all_to_all.59, f32[2,512,512]{2,1,0:T(8,128)S(1)} %copy-done), kind=kOutput, calls=%fused_computation.4 | convolution fusion | flops 402653184 | bytes 2621440 | tf_op jit(solution)/shard_map/sij,sabj->sabi/dot_general | solution.py:57
  55.0 0.4 collective-permute-start.10
  55.4 1.4 %collective-permute-start.11 = (f32[2,16,4,128]{3,1,2,0:T(8,128)S(1)}, f32[2,16,4,128]{3,1,2,0:T(8,128)S(1)}, u32[]{:S(2)}, u32[]{:S(2)}) collective-permute-start(f32[2,16,4,128]{3,1,2,0:T(8,128)S(1)} %get-tuple-element.24), channel_id=1, source_target_pairs={{0,3},{1,2},{2,1},{3,0},{4,7},{5,6},{6,5},{7,4},{8,11},{9,10},{10,... | collective-permute-start | bytes 196616 | tf_op jit(solution)/shard_map/ppermute | solution.py:73
  56.9 3.0 %collective-permute-done.10 = f32[2,16,4,128]{3,1,2,0:T(8,128)S(1)} collective-permute-done((f32[2,16,4,128]{3,1,2,0:T(8,128)S(1)}, f32[2,16,4,128]{3,1,2,0:T(8,128)S(1)}, u32[]{:S(2)}, u32[]{:S(2)}) %collective-permute-start.10) | collective-permute-done | bytes 65568 | tf_op jit(solution)/shard_map/ppermute | solution.py:73
  60.0 0.5 collective-permute-done.11
  60.5 1.6 %collective-permute-start.12 = (f32[2,1,16,128]{3,1,0,2:T(1,128)S(1)}, f32[2,1,16,128]{3,1,0,2:T(1,128)S(1)}, u32[]{:S(2)}, u32[]{:S(2)}) collective-permute-start(f32[2,1,16,128]{3,1,0,2:T(1,128)S(1)} %get-tuple-element.22), channel_id=1, source_target_pairs={{0,4},{1,5},{2,6},{3,7},{8,12},{9,13},{10,14},{11,15},{16,20},{17,... | collective-permute-start | bytes 49160 | tf_op jit(solution)/shard_map/ppermute | solution.py:18
  62.2 1.3 collective-permute-start.13
  63.6 4.2 %collective-permute-done.13 = f32[2,1,16,128]{3,1,0,2:T(1,128)S(1)} collective-permute-done((f32[2,1,16,128]{3,1,0,2:T(1,128)S(1)}, f32[2,1,16,128]{3,1,0,2:T(1,128)S(1)}, u32[]{:S(2)}, u32[]{:S(2)}) %collective-permute-start.13) | collective-permute-done | bytes 16416 | tf_op jit(solution)/shard_map/ppermute | solution.py:20
  67.9 0.3 fusion.27
  68.2 8.4 %all_to_all.73 = f32[2,16,16,128]{3,1,0,2:T(8,128)S(1)} all-to-all(f32[2,16,16,128]{3,1,0,2:T(8,128)S(1)} %fusion.27), channel_id=1, replica_groups=mesh['img'=4,'gx'=2,'gz'=4] {'gz'}, dimensions={2} | all-to-all | bytes 524288 | tf_op jit(solution)/shard_map/all_to_all | solution.py:60
  76.6 0.2 copy.98
  76.8 0.1 all_to_all.63
  76.9 2.1 %fusion.2 = f32[2,16,4,512]{3,1,2,0:T(8,128)S(1)} fusion(f32[2,16,4,512]{3,1,2,0:T(8,128)S(1)} %all_to_all.63, f32[2,512,512]{2,1,0:T(8,128)S(1)} %copy-done), kind=kOutput, calls=%fused_computation.2 | convolution fusion | flops 402653184 | bytes 2621440 | tf_op jit(solution)/shard_map/sij,sabj->sabi/dot_general | solution.py:57
  79.2 0.4 collective-permute-start.15
  79.6 1.4 %collective-permute-start.16 = (f32[2,16,4,128]{3,1,2,0:T(8,128)S(1)}, f32[2,16,4,128]{3,1,2,0:T(8,128)S(1)}, u32[]{:S(2)}, u32[]{:S(2)}) collective-permute-start(f32[2,16,4,128]{3,1,2,0:T(8,128)S(1)} %get-tuple-element.16), channel_id=1, source_target_pairs={{0,3},{1,2},{2,1},{3,0},{4,7},{5,6},{6,5},{7,4},{8,11},{9,10},{10,... | collective-permute-start | bytes 196616 | tf_op jit(solution)/shard_map/ppermute | solution.py:73
  81.1 3.0 %collective-permute-done.15 = f32[2,16,4,128]{3,1,2,0:T(8,128)S(1)} collective-permute-done((f32[2,16,4,128]{3,1,2,0:T(8,128)S(1)}, f32[2,16,4,128]{3,1,2,0:T(8,128)S(1)}, u32[]{:S(2)}, u32[]{:S(2)}) %collective-permute-start.15) | collective-permute-done | bytes 65568 | tf_op jit(solution)/shard_map/ppermute | solution.py:73
  84.1 0.5 collective-permute-done.16
  84.7 1.6 %collective-permute-start.17 = (f32[2,1,16,128]{3,1,0,2:T(1,128)S(1)}, f32[2,1,16,128]{3,1,0,2:T(1,128)S(1)}, u32[]{:S(2)}, u32[]{:S(2)}) collective-permute-start(f32[2,1,16,128]{3,1,0,2:T(1,128)S(1)} %get-tuple-element.14), channel_id=1, source_target_pairs={{0,4},{1,5},{2,6},{3,7},{8,12},{9,13},{10,14},{11,15},{16,20},{17,... | collective-permute-start | bytes 49160 | tf_op jit(solution)/shard_map/ppermute | solution.py:18
  86.3 1.3 collective-permute-start.18
  87.7 4.2 %collective-permute-done.18 = f32[2,1,16,128]{3,1,0,2:T(1,128)S(1)} collective-permute-done((f32[2,1,16,128]{3,1,0,2:T(1,128)S(1)}, f32[2,1,16,128]{3,1,0,2:T(1,128)S(1)}, u32[]{:S(2)}, u32[]{:S(2)}) %collective-permute-start.18) | collective-permute-done | bytes 16416 | tf_op jit(solution)/shard_map/ppermute | solution.py:20
  92.0 1.0 fusion.14
  93.0 3.6 %all-to-all-start.3 = ((f32[2,16,16,128]{3,1,0,2:T(8,128)}), f32[2,16,16,128]{3,1,0,2:T(8,128)S(1)}, u32[]{:S(2)}, u32[]{:S(2)}) async-start(f32[2,16,16,128]{3,1,0,2:T(8,128)} %fusion.14), calls=%async_computation.3 | async-start | bytes 524288 | tf_op jit(solution)/shard_map/all_to_all | solution.py:60
  96.6 0.6 select_reduce_fusion.1
  97.3 5.2 %all-to-all-done.3 = f32[2,16,16,128]{3,1,0,2:T(8,128)S(1)} async-done(((f32[2,16,16,128]{3,1,0,2:T(8,128)}), f32[2,16,16,128]{3,1,0,2:T(8,128)S(1)}, u32[]{:S(2)}, u32[]{:S(2)}) %all-to-all-start.3) | async-done | bytes 262176 | tf_op jit(solution)/shard_map/all_to_all | solution.py:60
  102.4 0.2 copy.97
  102.6 0.1 all_to_all.67
  102.7 2.1 %fusion = f32[2,16,4,512]{3,1,2,0:T(8,128)S(1)} fusion(f32[2,16,4,512]{3,1,2,0:T(8,128)S(1)} %all_to_all.67, f32[2,512,512]{2,1,0:T(8,128)S(1)} %copy-done), kind=kOutput, calls=%fused_computation | convolution fusion | flops 402653184 | bytes 2621440 | tf_op jit(solution)/shard_map/sij,sabj->sabi/dot_general | solution.py:57
  105.0 0.4 collective-permute-start.20
  105.4 1.4 %collective-permute-start.21 = (f32[2,16,4,128]{3,1,2,0:T(8,128)S(1)}, f32[2,16,4,128]{3,1,2,0:T(8,128)S(1)}, u32[]{:S(2)}, u32[]{:S(2)}) collective-permute-start(f32[2,16,4,128]{3,1,2,0:T(8,128)S(1)} %get-tuple-element.8), channel_id=1, source_target_pairs={{0,3},{1,2},{2,1},{3,0},{4,7},{5,6},{6,5},{7,4},{8,11},{9,10},{10,... | collective-permute-start | bytes 196616 | tf_op jit(solution)/shard_map/ppermute | solution.py:73
  106.9 3.0 %collective-permute-done.20 = f32[2,16,4,128]{3,1,2,0:T(8,128)S(1)} collective-permute-done((f32[2,16,4,128]{3,1,2,0:T(8,128)S(1)}, f32[2,16,4,128]{3,1,2,0:T(8,128)S(1)}, u32[]{:S(2)}, u32[]{:S(2)}) %collective-permute-start.20) | collective-permute-done | bytes 65568 | tf_op jit(solution)/shard_map/ppermute | solution.py:73
  110.0 0.5 collective-permute-done.21
  110.5 1.3 collective-permute-start.22
  111.8 1.3 collective-permute-start.23
  113.1 4.6 %collective-permute-start.24 = (f32[2,16,16,128]{3,1,0,2:T(8,128)S(1)}, f32[2,16,16,128]{3,1,0,2:T(8,128)S(1)}, u32[]{:S(2)}, u32[]{:S(2)}) collective-permute-start(f32[2,16,16,128]{3,1,0,2:T(8,128)S(1)} %copy_dynamic-update-slice_fusion), channel_id=1, source_target_pairs={{8,0},{16,8},{24,16},{9,1},{17,9},{25,17},{10,2},{18,10},{26,18},{... | collective-permute-start | bytes 786440 | tf_op jit(solution)/shard_map/ppermute | solution.py:30
  117.6 5.5 %collective-permute-start.25 = (f32[2,16,16,128]{3,1,0,2:T(8,128)S(1)}, f32[2,16,16,128]{3,1,0,2:T(8,128)S(1)}, u32[]{:S(2)}, u32[]{:S(2)}) collective-permute-start(f32[2,16,16,128]{3,1,0,2:T(8,128)S(1)} %copy_dynamic-update-slice_fusion), channel_id=1, source_target_pairs={{16,0},{24,8},{17,1},{25,9},{18,2},{26,10},{19,3},{27,11},{20,4},{... | collective-permute-start | bytes 786440 | tf_op jit(solution)/shard_map/ppermute | solution.py:30
  128.2 0.7 fusion.77
  141.3 0.1 add_bitcast_fusion
  141.5 0.9 copy.58
  (67 shorter events, 1.7 us)
Async XLA Ops:
  0.0 27.9 %copy-start = (f32[2,512,512]{2,1,0:T(8,128)S(1)}, f32[2,512,512]{2,1,0:T(8,128)}, u32[]{:S(2)}) copy-start(f32[2,512,512]{2,1,0:T(8,128)} %param.7) | copy-start | bytes 6291460
  0.0 17.1 %copy-start.1 = (f32[2,16,16,128]{3,2,1,0:T(8,128)S(1)}, f32[2,16,16,128]{3,2,1,0:T(8,128)}, u32[]{:S(2)}) copy-start(f32[2,16,16,128]{3,2,1,0:T(8,128)} %param.6) | copy-start | bytes 786436
  0.9 16.1 %collective-permute-start = (f32[2,1,16,128]{3,1,0,2:T(1,128)S(1)}, f32[2,1,16,128]{3,1,0,2:T(1,128)S(1)}, u32[]{:S(2)}, u32[]{:S(2)}) collective-permute-start(f32[2,1,16,128]{3,1,0,2:T(1,128)S(1)} %copy.29), channel_id=1, source_target_pairs={{0,4},{1,5},{2,6},{3,7},{8,12},{9,13},{10,14},{11,15},{16,20},{17,... | collective-permute-start | bytes 49160 | tf_op jit(solution)/shard_map/ppermute | solution.py:18
  4.4 12.6 %collective-permute-start.2 = (f32[2,1,16,128]{3,1,0,2:T(1,128)S(1)}, f32[2,1,16,128]{3,1,0,2:T(1,128)S(1)}, u32[]{:S(2)}, u32[]{:S(2)}) collective-permute-start(f32[2,1,16,128]{3,1,0,2:T(1,128)S(1)} %copy.32), channel_id=1, source_target_pairs={{4,0},{5,1},{6,2},{7,3},{12,8},{13,9},{14,10},{15,11},{20,16},{21,... | collective-permute-start | bytes 49160 | tf_op jit(solution)/shard_map/ppermute | solution.py:20
  6.7 8.0 %collective-permute-start.1 = (f32[2,1,16,128]{3,1,0,2:T(1,128)S(1)}, f32[2,1,16,128]{3,1,0,2:T(1,128)S(1)}, u32[]{:S(2)}, u32[]{:S(2)}) collective-permute-start(f32[2,1,16,128]{3,1,0,2:T(1,128)S(1)} %get-tuple-element.42), channel_id=1, source_target_pairs={{0,4},{1,5},{2,6},{3,7},{8,12},{9,13},{10,14},{11,15},{16,20},{17,... | collective-permute-start | bytes 49160 | tf_op jit(solution)/shard_map/ppermute | solution.py:18
  11.3 5.6 %collective-permute-start.3 = (f32[2,1,16,128]{3,1,0,2:T(1,128)S(1)}, f32[2,1,16,128]{3,1,0,2:T(1,128)S(1)}, u32[]{:S(2)}, u32[]{:S(2)}) collective-permute-start(f32[2,1,16,128]{3,1,0,2:T(1,128)S(1)} %get-tuple-element.43), channel_id=1, source_target_pairs={{4,0},{5,1},{6,2},{7,3},{12,8},{13,9},{14,10},{15,11},{20,16},{21,... | collective-permute-start | bytes 49160 | tf_op jit(solution)/shard_map/ppermute | solution.py:20
  18.2 9.4 %all-to-all-start = ((f32[2,16,16,128]{3,1,0,2:T(8,128)}), f32[2,16,16,128]{3,1,0,2:T(8,128)S(1)}, u32[]{:S(2)}, u32[]{:S(2)}) async-start(f32[2,16,16,128]{3,1,0,2:T(8,128)} %get-tuple-element.5), calls=%async_computation | async-start | bytes 524288 | tf_op jit(solution)/shard_map/all_to_all | solution.py:60
  30.1 2.0 %collective-permute-start.4 = (f32[2,16,4,128]{3,1,2,0:T(8,128)S(1)}, f32[2,16,4,128]{3,1,2,0:T(8,128)S(1)}, u32[]{:S(2)}, u32[]{:S(2)}) collective-permute-start(f32[2,16,4,128]{3,1,2,0:T(8,128)S(1)} %get-tuple-element.34), channel_id=1, source_target_pairs={{0,1},{1,0},{2,3},{3,2},{4,5},{5,4},{6,7},{7,6},{8,9},{9,8},{10,11... | collective-permute-start | bytes 196616 | tf_op jit(solution)/shard_map/ppermute | solution.py:73
  30.1 5.0 %collective-permute-start.5 = (f32[2,16,4,128]{3,1,2,0:T(8,128)S(1)}, f32[2,16,4,128]{3,1,2,0:T(8,128)S(1)}, u32[]{:S(2)}, u32[]{:S(2)}) collective-permute-start(f32[2,16,4,128]{3,1,2,0:T(8,128)S(1)} %get-tuple-element.33), channel_id=1, source_target_pairs={{0,2},{1,3},{2,0},{3,1},{4,6},{5,7},{6,4},{7,5},{8,10},{9,11},{10,... | collective-permute-start | bytes 196616 | tf_op jit(solution)/shard_map/ppermute | solution.py:73
  30.6 5.0 %collective-permute-start.6 = (f32[2,16,4,128]{3,1,2,0:T(8,128)S(1)}, f32[2,16,4,128]{3,1,2,0:T(8,128)S(1)}, u32[]{:S(2)}, u32[]{:S(2)}) collective-permute-start(f32[2,16,4,128]{3,1,2,0:T(8,128)S(1)} %get-tuple-element.32), channel_id=1, source_target_pairs={{0,3},{1,2},{2,1},{3,0},{4,7},{5,6},{6,5},{7,4},{8,11},{9,10},{10,... | collective-permute-start | bytes 196616 | tf_op jit(solution)/shard_map/ppermute | solution.py:73
  35.6 3.8 %collective-permute-start.7 = (f32[2,1,16,128]{3,1,0,2:T(1,128)S(1)}, f32[2,1,16,128]{3,1,0,2:T(1,128)S(1)}, u32[]{:S(2)}, u32[]{:S(2)}) collective-permute-start(f32[2,1,16,128]{3,1,0,2:T(1,128)S(1)} %get-tuple-element.30), channel_id=1, source_target_pairs={{0,4},{1,5},{2,6},{3,7},{8,12},{9,13},{10,14},{11,15},{16,20},{17,... | collective-permute-start | bytes 49160 | tf_op jit(solution)/shard_map/ppermute | solution.py:18
  38.0 5.6 %collective-permute-start.8 = (f32[2,1,16,128]{3,1,0,2:T(1,128)S(1)}, f32[2,1,16,128]{3,1,0,2:T(1,128)S(1)}, u32[]{:S(2)}, u32[]{:S(2)}) collective-permute-start(f32[2,1,16,128]{3,1,0,2:T(1,128)S(1)} %get-tuple-element.31), channel_id=1, source_target_pairs={{4,0},{5,1},{6,2},{7,3},{12,8},{13,9},{14,10},{15,11},{20,16},{21,... | collective-permute-start | bytes 49160 | tf_op jit(solution)/shard_map/ppermute | solution.py:20
  54.9 2.0 %collective-permute-start.9 = (f32[2,16,4,128]{3,1,2,0:T(8,128)S(1)}, f32[2,16,4,128]{3,1,2,0:T(8,128)S(1)}, u32[]{:S(2)}, u32[]{:S(2)}) collective-permute-start(f32[2,16,4,128]{3,1,2,0:T(8,128)S(1)} %get-tuple-element.26), channel_id=1, source_target_pairs={{0,1},{1,0},{2,3},{3,2},{4,5},{5,4},{6,7},{7,6},{8,9},{9,8},{10,11... | collective-permute-start | bytes 196616 | tf_op jit(solution)/shard_map/ppermute | solution.py:73
  55.0 5.0 %collective-permute-start.10 = (f32[2,16,4,128]{3,1,2,0:T(8,128)S(1)}, f32[2,16,4,128]{3,1,2,0:T(8,128)S(1)}, u32[]{:S(2)}, u32[]{:S(2)}) collective-permute-start(f32[2,16,4,128]{3,1,2,0:T(8,128)S(1)} %get-tuple-element.25), channel_id=1, source_target_pairs={{0,2},{1,3},{2,0},{3,1},{4,6},{5,7},{6,4},{7,5},{8,10},{9,11},{10,... | collective-permute-start | bytes 196616 | tf_op jit(solution)/shard_map/ppermute | solution.py:73
  55.4 5.0 %collective-permute-start.11 = (f32[2,16,4,128]{3,1,2,0:T(8,128)S(1)}, f32[2,16,4,128]{3,1,2,0:T(8,128)S(1)}, u32[]{:S(2)}, u32[]{:S(2)}) collective-permute-start(f32[2,16,4,128]{3,1,2,0:T(8,128)S(1)} %get-tuple-element.24), channel_id=1, source_target_pairs={{0,3},{1,2},{2,1},{3,0},{4,7},{5,6},{6,5},{7,4},{8,11},{9,10},{10,... | collective-permute-start | bytes 196616 | tf_op jit(solution)/shard_map/ppermute | solution.py:73
  60.5 3.1 %collective-permute-start.12 = (f32[2,1,16,128]{3,1,0,2:T(1,128)S(1)}, f32[2,1,16,128]{3,1,0,2:T(1,128)S(1)}, u32[]{:S(2)}, u32[]{:S(2)}) collective-permute-start(f32[2,1,16,128]{3,1,0,2:T(1,128)S(1)} %get-tuple-element.22), channel_id=1, source_target_pairs={{0,4},{1,5},{2,6},{3,7},{8,12},{9,13},{10,14},{11,15},{16,20},{17,... | collective-permute-start | bytes 49160 | tf_op jit(solution)/shard_map/ppermute | solution.py:18
  62.2 5.6 %collective-permute-start.13 = (f32[2,1,16,128]{3,1,0,2:T(1,128)S(1)}, f32[2,1,16,128]{3,1,0,2:T(1,128)S(1)}, u32[]{:S(2)}, u32[]{:S(2)}) collective-permute-start(f32[2,1,16,128]{3,1,0,2:T(1,128)S(1)} %get-tuple-element.23), channel_id=1, source_target_pairs={{4,0},{5,1},{6,2},{7,3},{12,8},{13,9},{14,10},{15,11},{20,16},{21,... | collective-permute-start | bytes 49160 | tf_op jit(solution)/shard_map/ppermute | solution.py:20
  79.1 2.0 %collective-permute-start.14 = (f32[2,16,4,128]{3,1,2,0:T(8,128)S(1)}, f32[2,16,4,128]{3,1,2,0:T(8,128)S(1)}, u32[]{:S(2)}, u32[]{:S(2)}) collective-permute-start(f32[2,16,4,128]{3,1,2,0:T(8,128)S(1)} %get-tuple-element.18), channel_id=1, source_target_pairs={{0,1},{1,0},{2,3},{3,2},{4,5},{5,4},{6,7},{7,6},{8,9},{9,8},{10,11... | collective-permute-start | bytes 196616 | tf_op jit(solution)/shard_map/ppermute | solution.py:73
  79.2 5.0 %collective-permute-start.15 = (f32[2,16,4,128]{3,1,2,0:T(8,128)S(1)}, f32[2,16,4,128]{3,1,2,0:T(8,128)S(1)}, u32[]{:S(2)}, u32[]{:S(2)}) collective-permute-start(f32[2,16,4,128]{3,1,2,0:T(8,128)S(1)} %get-tuple-element.17), channel_id=1, source_target_pairs={{0,2},{1,3},{2,0},{3,1},{4,6},{5,7},{6,4},{7,5},{8,10},{9,11},{10,... | collective-permute-start | bytes 196616 | tf_op jit(solution)/shard_map/ppermute | solution.py:73
  79.6 5.0 %collective-permute-start.16 = (f32[2,16,4,128]{3,1,2,0:T(8,128)S(1)}, f32[2,16,4,128]{3,1,2,0:T(8,128)S(1)}, u32[]{:S(2)}, u32[]{:S(2)}) collective-permute-start(f32[2,16,4,128]{3,1,2,0:T(8,128)S(1)} %get-tuple-element.16), channel_id=1, source_target_pairs={{0,3},{1,2},{2,1},{3,0},{4,7},{5,6},{6,5},{7,4},{8,11},{9,10},{10,... | collective-permute-start | bytes 196616 | tf_op jit(solution)/shard_map/ppermute | solution.py:73
  84.1 12.5 %copy-start.3 = (s32[4]{0:T(128)S(1)}, s32[4]{0:T(128)}, u32[]{:S(2)}) copy-start(s32[4]{0:T(128)} %param.8) | copy-start | bytes 52
  84.7 3.1 %collective-permute-start.17 = (f32[2,1,16,128]{3,1,0,2:T(1,128)S(1)}, f32[2,1,16,128]{3,1,0,2:T(1,128)S(1)}, u32[]{:S(2)}, u32[]{:S(2)}) collective-permute-start(f32[2,1,16,128]{3,1,0,2:T(1,128)S(1)} %get-tuple-element.14), channel_id=1, source_target_pairs={{0,4},{1,5},{2,6},{3,7},{8,12},{9,13},{10,14},{11,15},{16,20},{17,... | collective-permute-start | bytes 49160 | tf_op jit(solution)/shard_map/ppermute | solution.py:18
  86.3 5.6 %collective-permute-start.18 = (f32[2,1,16,128]{3,1,0,2:T(1,128)S(1)}, f32[2,1,16,128]{3,1,0,2:T(1,128)S(1)}, u32[]{:S(2)}, u32[]{:S(2)}) collective-permute-start(f32[2,1,16,128]{3,1,0,2:T(1,128)S(1)} %get-tuple-element.15), channel_id=1, source_target_pairs={{4,0},{5,1},{6,2},{7,3},{12,8},{13,9},{14,10},{15,11},{20,16},{21,... | collective-permute-start | bytes 49160 | tf_op jit(solution)/shard_map/ppermute | solution.py:20
  93.0 9.4 %all-to-all-start.3 = ((f32[2,16,16,128]{3,1,0,2:T(8,128)}), f32[2,16,16,128]{3,1,0,2:T(8,128)S(1)}, u32[]{:S(2)}, u32[]{:S(2)}) async-start(f32[2,16,16,128]{3,1,0,2:T(8,128)} %fusion.14), calls=%async_computation.3 | async-start | bytes 524288 | tf_op jit(solution)/shard_map/all_to_all | solution.py:60
  102.7 25.4 %copy-start.2 = (f32[4,4]{1,0:T(4,128)S(1)}, f32[4,4]{1,0:T(4,128)}, u32[]{:S(2)}) copy-start(f32[4,4]{1,0:T(4,128)} %param.9) | copy-start | bytes 196
  104.9 2.0 %collective-permute-start.19 = (f32[2,16,4,128]{3,1,2,0:T(8,128)S(1)}, f32[2,16,4,128]{3,1,2,0:T(8,128)S(1)}, u32[]{:S(2)}, u32[]{:S(2)}) collective-permute-start(f32[2,16,4,128]{3,1,2,0:T(8,128)S(1)} %get-tuple-element.10), channel_id=1, source_target_pairs={{0,1},{1,0},{2,3},{3,2},{4,5},{5,4},{6,7},{7,6},{8,9},{9,8},{10,11... | collective-permute-start | bytes 196616 | tf_op jit(solution)/shard_map/ppermute | solution.py:73
  105.0 5.0 %collective-permute-start.20 = (f32[2,16,4,128]{3,1,2,0:T(8,128)S(1)}, f32[2,16,4,128]{3,1,2,0:T(8,128)S(1)}, u32[]{:S(2)}, u32[]{:S(2)}) collective-permute-start(f32[2,16,4,128]{3,1,2,0:T(8,128)S(1)} %get-tuple-element.9), channel_id=1, source_target_pairs={{0,2},{1,3},{2,0},{3,1},{4,6},{5,7},{6,4},{7,5},{8,10},{9,11},{10,... | collective-permute-start | bytes 196616 | tf_op jit(solution)/shard_map/ppermute | solution.py:73
  105.4 5.0 %collective-permute-start.21 = (f32[2,16,4,128]{3,1,2,0:T(8,128)S(1)}, f32[2,16,4,128]{3,1,2,0:T(8,128)S(1)}, u32[]{:S(2)}, u32[]{:S(2)}) collective-permute-start(f32[2,16,4,128]{3,1,2,0:T(8,128)S(1)} %get-tuple-element.8), channel_id=1, source_target_pairs={{0,3},{1,2},{2,1},{3,0},{4,7},{5,6},{6,5},{7,4},{8,11},{9,10},{10,... | collective-permute-start | bytes 196616 | tf_op jit(solution)/shard_map/ppermute | solution.py:73
  110.5 30.8 %collective-permute-start.22 = (f32[2,16,16,128]{3,1,0,2:T(8,128)S(1)}, f32[2,16,16,128]{3,1,0,2:T(8,128)S(1)}, u32[]{:S(2)}, u32[]{:S(2)}) collective-permute-start(f32[2,16,16,128]{3,1,0,2:T(8,128)S(1)} %copy_dynamic-update-slice_fusion), channel_id=1, source_target_pairs={{0,16},{8,24},{1,17},{9,25},{2,18},{10,26},{3,19},{11,27},{4,20},{... | collective-permute-start | bytes 786440 | tf_op jit(solution)/shard_map/ppermute | solution.py:30
  111.8 29.5 %collective-permute-start.23 = (f32[2,16,16,128]{3,1,0,2:T(8,128)S(1)}, f32[2,16,16,128]{3,1,0,2:T(8,128)S(1)}, u32[]{:S(2)}, u32[]{:S(2)}) collective-permute-start(f32[2,16,16,128]{3,1,0,2:T(8,128)S(1)} %copy_dynamic-update-slice_fusion), channel_id=1, source_target_pairs={{0,8},{8,16},{16,24},{1,9},{9,17},{17,25},{2,10},{10,18},{18,26},{... | collective-permute-start | bytes 786440 | tf_op jit(solution)/shard_map/ppermute | solution.py:30
  113.1 28.2 %collective-permute-start.24 = (f32[2,16,16,128]{3,1,0,2:T(8,128)S(1)}, f32[2,16,16,128]{3,1,0,2:T(8,128)S(1)}, u32[]{:S(2)}, u32[]{:S(2)}) collective-permute-start(f32[2,16,16,128]{3,1,0,2:T(8,128)S(1)} %copy_dynamic-update-slice_fusion), channel_id=1, source_target_pairs={{8,0},{16,8},{24,16},{9,1},{17,9},{25,17},{10,2},{18,10},{26,18},{... | collective-permute-start | bytes 786440 | tf_op jit(solution)/shard_map/ppermute | solution.py:30
  117.6 23.7 %collective-permute-start.25 = (f32[2,16,16,128]{3,1,0,2:T(8,128)S(1)}, f32[2,16,16,128]{3,1,0,2:T(8,128)S(1)}, u32[]{:S(2)}, u32[]{:S(2)}) collective-permute-start(f32[2,16,16,128]{3,1,0,2:T(8,128)S(1)} %copy_dynamic-update-slice_fusion), channel_id=1, source_target_pairs={{16,0},{24,8},{17,1},{25,9},{18,2},{26,10},{19,3},{27,11},{20,4},{... | collective-permute-start | bytes 786440 | tf_op jit(solution)/shard_map/ppermute | solution.py:30
